TPU v7x, 128 devices: a whole 4x4x4 slice. The times are simulated.
128 devices in a mesh: area: 8 (over y, core), depth: 16 (over x, z).
Axes of the slice: x: 4, y: 4, z: 4, core: 2. Of those that a mesh axis runs over, the one named last changes fastest.
Arguments:
- field: float32 [512, 512, 512], P('depth', 'area'), may hold values from -6 to 6
- materials: int32 [512, 512, 512], P('depth', 'area'), may hold values from 0 to 15
- tf_table: float32 [4, 16], replicated, may hold values from 0 to 1, as said below
- view_order: int32 [2, 16], replicated, may hold values from 0 to 15, each once within a row
- shear_offset: int32 [16], replicated, may hold values from 0 to 63, as said below
Outputs:
- image: float32 [2, 4, 512, 512], P(None, None, ('area', 'depth'))
Inputs may be any that keep to these rules, and one draw needn't show every extreme that they name: `shear_offset`: every entry lies in 0 to 63; some layer has offset 0 and some layer has offset 64 - 1. `view_order`: each row is a permutation of the depth layers. `tf_table`: the colour rows lie in 0.05 to 0.6; the opacity row lies in 0.02 / 32 to 0.5 / 32.
All inputs are finite; a program needn't handle non-finite values.
Results may differ from a plain program's by a relative error of at most 0.0003.
Values sent between devices are 32-bit elements; how exact they have to be, the bound alone decides.
A program may use at most 128 MiB of HBM per device.

v0:
```python
import functools

import jax
import jax.numpy as jnp
from jax import lax
from jax.experimental import pallas as pl
from jax.experimental.pallas import tpu as pltpu
from jax.sharding import PartitionSpec as P

MESH = pl.DeviceIdType.MESH
LANES = 128
SUB = 8
EXP_SCALE = -0.25 * 1.4426950408889634


def sublane_gather(table, index):
    dims = lax.GatherDimensionNumbers(
        offset_dims=(),
        collapsed_slice_dims=(0,),
        start_index_map=(0,),
        operand_batching_dims=(1,),
        start_indices_batching_dims=(1,),
    )
    return lax.gather(
        table, index[..., None], dims, (1, 1), mode=lax.GatherScatterMode.PROMISE_IN_BOUNDS
    )


def kernel(
    n_area,
    n_depth,
    field_hbm,
    mat_hbm,
    tf_hbm,
    order_hbm,
    shear_hbm,
    out_ref,
    F,
    M,
    tf_s,
    order_s,
    shear_s,
    edge_out,
    edge_in,
    state,
    own,
    near,
    window,
    send,
    recv,
    load_sem,
    small_sem,
    halo_send,
    halo_recv,
    shear_send,
    shear_recv,
    a2a_send,
    a2a_recv,
):
    planes, rows, columns = field_hbm.shape
    blocks = columns // LANES
    tiles = rows // SUB
    part = rows // n_depth
    area, depth = lax.axis_index("area"), lax.axis_index("depth")
    zero = jnp.zeros((SUB, LANES), jnp.float32)

    for b in range(blocks):
        pltpu.make_async_copy(
            field_hbm.at[:, :, pl.ds(b * LANES, LANES)],
            F.at[b + 1, pl.ds(1, planes), pl.ds(SUB, rows)],
            load_sem.at[b],
        ).start()
    for b in range(blocks):
        pltpu.make_async_copy(
            mat_hbm.at[:, :, pl.ds(b * LANES, LANES)], M.at[b], load_sem.at[blocks + b]
        ).start()
    small = [
        pltpu.make_async_copy(src, dst, small_sem.at[i])
        for i, (src, dst) in enumerate(
            ((tf_hbm, tf_s), (order_hbm, order_s), (shear_hbm, shear_s))
        )
    ]
    for copy in small:
        copy.start()

    def wait_field(b):
        pltpu.make_async_copy(
            F.at[b + 1, pl.ds(1, planes), pl.ds(SUB, rows)],
            F.at[b + 1, pl.ds(1, planes), pl.ds(SUB, rows)],
            load_sem.at[b],
        ).wait()

    def wait_mat(b):
        pltpu.make_async_copy(M.at[b], M.at[b], load_sem.at[blocks + b]).wait()

    barrier = pltpu.get_barrier_semaphore()

    def greet(i, _):
        peer = lax.rem(depth + i, n_depth)
        pl.semaphore_signal(barrier, inc=1, device_id={"depth": peer}, device_id_type=MESH)
        return 0

    lax.fori_loop(1, n_depth, greet, 0)

    @pl.when(area > 0)
    def _():
        pl.semaphore_signal(barrier, inc=1, device_id={"area": area - 1}, device_id_type=MESH)

    @pl.when(area < n_area - 1)
    def _():
        pl.semaphore_signal(barrier, inc=1, device_id={"area": area + 1}, device_id_type=MESH)

    def clear(k, _):
        for r in range(tiles + 2):
            F[0, k, pl.ds(r * SUB, SUB), :] = zero
            F[blocks + 1, k, pl.ds(r * SUB, SUB), :] = zero
        return 0

    lax.fori_loop(0, planes + 2, clear, 0)

    def clear_plane(at):
        for b in range(blocks):
            for r in range(tiles):
                F[b + 1, at, pl.ds(SUB + r * SUB, SUB), :] = zero

    @pl.when(depth == 0)
    def _():
        clear_plane(0)

    @pl.when(depth == n_depth - 1)
    def _():
        clear_plane(planes + 1)

    @pl.when(jnp.logical_and(area > 0, area < n_area - 1))
    def _():
        pl.semaphore_wait(barrier, n_depth - 1 + 2)

    @pl.when(jnp.logical_or(area == 0, area == n_area - 1))
    def _():
        pl.semaphore_wait(barrier, n_depth - 1 + 1)

    def plane_copy(b, src, dst, slot, peer):
        return pltpu.make_async_remote_copy(
            src_ref=field_hbm.at[src, :, pl.ds(b * LANES, LANES)],
            dst_ref=F.at[b + 1, dst, pl.ds(SUB, rows)],
            send_sem=halo_send.at[slot],
            recv_sem=halo_recv.at[slot],
            device_id={"depth": peer},
            device_id_type=MESH,
        )

    @pl.when(depth < n_depth - 1)
    def _():
        for b in range(blocks):
            plane_copy(b, planes - 1, 0, 0, depth + 1).start()

    @pl.when(depth > 0)
    def _():
        for b in range(blocks):
            plane_copy(b, 0, planes + 1, 1, depth - 1).start()

    for b in range(blocks):
        wait_field(b)
        for k in range(planes):
            edge_out[0, b, pl.ds(k, 1), :] = F[b + 1, k + 1, pl.ds(SUB, 1), :]
            edge_out[1, b, pl.ds(k, 1), :] = F[b + 1, k + 1, pl.ds(SUB + rows - 1, 1), :]

    def edge_copy(src, peer):
        return pltpu.make_async_remote_copy(
            src_ref=edge_out.at[src],
            dst_ref=edge_in.at[1 - src],
            send_sem=halo_send.at[2 + src],
            recv_sem=halo_recv.at[2 + src],
            device_id={"area": peer},
            device_id_type=MESH,
        )

    @pl.when(area < n_area - 1)
    def _():
        edge_copy(1, area + 1).start()

    @pl.when(area > 0)
    def _():
        edge_copy(0, area - 1).start()

    for copy in small:
        copy.wait()
    sub_id = lax.broadcasted_iota(jnp.int32, (SUB, LANES), 0)
    lane_id = lax.broadcasted_iota(jnp.int32, (SUB, LANES), 1)
    is_first, is_last = lane_id == 0, lane_id == LANES - 1
    table = []
    for channel in range(4):
        halves = []
        for half in range(2):
            values = jnp.full((SUB, LANES), tf_s[channel, half * SUB], jnp.float32)
            for entry in range(1, SUB):
                values = jnp.where(sub_id == entry, tf_s[channel, half * SUB + entry], values)
            halves.append(values)
        table.append(halves)

    def cells(b, k, row):
        mid = pl.ds(pl.multiple_of(row + SUB, SUB), SUB)
        c = F[b + 1, k + 1, mid, :]
        gz = F[b + 1, k + 2, mid, :] - F[b + 1, k, mid, :]
        gy = F[b + 1, k + 1, pl.ds(row + SUB + 1, SUB), :] - F[b + 1, k + 1, pl.ds(row + SUB - 1, SUB), :]
        before = pltpu.roll(jnp.where(is_last, F[b, k + 1, mid, :], c), 1, 1)
        after = pltpu.roll(jnp.where(is_first, F[b + 2, k + 1, mid, :], c), LANES - 1, 1)
        gx = after - before
        gm2 = 0.25 * (gz * gz + gy * gy + gx * gx)
        lit = jnp.abs(0.168 * gz + 0.21 * gy + 0.224 * gx)
        shade = 0.3 + lit * lax.rsqrt(gm2 + 1.0)
        m = M[b, k, pl.ds(pl.multiple_of(row, SUB), SUB), :]
        upper, index = m > SUB - 1, m & (SUB - 1)
        looked = [
            jnp.where(upper, sublane_gather(hi, index), sublane_gather(lo, index))
            for lo, hi in table
        ]
        a = looked[3] * (1.0 - jnp.exp2(EXP_SCALE * (c * c + gm2)))
        return looked[:3], shade * a, 1.0 - a

    def interior(b, tile):
        row = tile * SUB
        through = zero + 1.0
        front, back = [zero] * 3, [zero] * 3
        for k in range(1, planes - 1):
            colour, sa, keep = cells(b, k, row)
            weight = through * sa
            front = [f + t * weight for f, t in zip(front, colour)]
            back = [f * keep + t * sa for f, t in zip(back, colour)]
            through = through * keep
        for i, value in enumerate([through, *front, *back]):
            state[b, i, pl.ds(pl.multiple_of(row, SUB), SUB), :] = value

    def ends(b, tile):
        row = tile * SUB
        at = pl.ds(pl.multiple_of(row, SUB), SUB)
        colour0, sa0, keep0 = cells(b, 0, row)
        colour1, sa1, keep1 = cells(b, planes - 1, row)
        through = state[b, 0, at, :]
        opacity = 1.0 - through * keep0 * keep1
        for i in range(4):
            if i == 3:
                first, second = opacity, opacity
            else:
                c0, c1 = colour0[i] * sa0, colour1[i] * sa1
                first = c0 + keep0 * (state[b, 1 + i, at, :] + through * c1)
                second = c1 + keep1 * (state[b, 4 + i, at, :] + through * c0)
            own[b, i, at, :] = second
            for half in range(SUB // part):
                send[0, b, tile * (SUB // part) + half, pl.ds(i * part, part), :] = first[
                    half * part : (half + 1) * part
                ]

    def send_view(view, b):
        def one(i, _):
            peer = lax.rem(depth + i, n_depth)
            pltpu.make_async_remote_copy(
                src_ref=send.at[view, b, peer],
                dst_ref=recv.at[view, b, depth],
                send_sem=a2a_send.at[view],
                recv_sem=a2a_recv.at[view],
                device_id={"depth": peer},
                device_id_type=MESH,
            ).start()
            return 0

        lax.fori_loop(1, n_depth, one, 0)
        recv[view, b, depth] = send[view, b, depth]

    def shear_copy(b):
        return pltpu.make_async_remote_copy(
            src_ref=own.at[b],
            dst_ref=near.at[b],
            send_sem=shear_send.at[b],
            recv_sem=shear_recv.at[b],
            device_id={"area": area + 1},
            device_id_type=MESH,
        )

    offset = shear_s[depth]

    def shear(b):
        @pl.when(area > 0)
        def _():
            pltpu.make_async_copy(near.at[b], near.at[b], shear_recv.at[b]).wait()
            for i in range(4):
                window[i, pl.ds(0, rows), :] = near[b, i]

        for i in range(4):
            window[i, pl.ds(rows, rows), :] = own[b, i]
        for tile in range(tiles):
            for i in range(4):
                moved = window[i, pl.ds(rows + tile * SUB - offset, SUB), :]
                for half in range(SUB // part):
                    send[1, b, tile * (SUB // part) + half, pl.ds(i * part, part), :] = moved[
                        half * part : (half + 1) * part
                    ]
        send_view(1, b)

    @pl.when(area == 0)
    def _():
        for i in range(4):
            for tile in range(tiles):
                window[i, pl.ds(tile * SUB, SUB), :] = zero

    inner = tiles - 2
    early = 2

    def first_pass(i, _):
        b = i // inner
        tile = 1 + i % inner

        @pl.when(tile == 1)
        def _():
            wait_mat(b)

        interior(b, tile)
        return 0

    lax.fori_loop(0, early * inner, first_pass, 0)

    @pl.when(depth > 0)
    def _():
        at = F.at[pl.ds(1, blocks), 0, pl.ds(SUB, rows)]
        pltpu.make_async_copy(at, at, halo_recv.at[0]).wait()

    @pl.when(depth < n_depth - 1)
    def _():
        at = F.at[pl.ds(1, blocks), planes + 1, pl.ds(SUB, rows)]
        pltpu.make_async_copy(at, at, halo_recv.at[1]).wait()

    @pl.when(area > 0)
    def _():
        pltpu.make_async_copy(edge_in.at[0], edge_in.at[0], halo_recv.at[3]).wait()
        for b in range(blocks):
            for k in range(planes):
                F[b + 1, k + 1, pl.ds(SUB - 1, 1), :] = edge_in[0, b, pl.ds(k, 1), :]

    @pl.when(area < n_area - 1)
    def _():
        pltpu.make_async_copy(edge_in.at[1], edge_in.at[1], halo_recv.at[2]).wait()
        for b in range(blocks):
            for k in range(planes):
                F[b + 1, k + 1, pl.ds(SUB + rows, 1), :] = edge_in[1, b, pl.ds(k, 1), :]

    @pl.when(area == 0)
    def _():
        for b in range(blocks):
            for k in range(planes):
                F[b + 1, k + 1, pl.ds(SUB - 1, 1), :] = zero[:1]

    @pl.when(area == n_area - 1)
    def _():
        for b in range(blocks):
            for k in range(planes):
                F[b + 1, k + 1, pl.ds(SUB + rows, 1), :] = zero[:1]

    def block(b, _):
        late = b // early

        @pl.when(b >= early)
        def _():
            wait_mat(b)

        def rest(t, _):
            interior(b, t * ((tiles - 1) - (tiles - 2) * late))
            return 0

        lax.fori_loop(0, 2 + inner * late, rest, 0)

        def finish(t, _):
            ends(b, 2 * t)
            ends(b, 2 * t + 1)
            return 0

        lax.fori_loop(0, tiles // 2, finish, 0)

        @pl.when(area < n_area - 1)
        def _():
            shear_copy(b).start()

        send_view(0, b)

        @pl.when(b > 0)
        def _():
            shear(b - 1)

        return 0

    lax.fori_loop(0, blocks, block, 0)
    shear(blocks - 1)

    for view in range(2):
        at = recv.at[view, :, pl.ds(0, n_depth - 1)]
        pltpu.make_async_copy(at, at, a2a_recv.at[view]).wait()

    low = sub_id < part
    for view in range(2):

        def compose(b, _):
            through = zero + 1.0
            total = [zero, zero]
            for k in range(n_depth):
                layer = order_s[view, k]
                one = recv[view, b, layer, pl.ds(0, SUB), :]
                two = recv[view, b, layer, pl.ds(SUB, SUB), :]
                total = [total[0] + through * one, total[1] + through * two]
                opacity = jnp.where(low, pltpu.roll(two, part, 0), two)
                through = through * (1.0 - opacity)
            columns_b = pl.ds(pl.multiple_of(b * LANES, LANES), LANES)
            out_ref[view, pl.ds(0, SUB), columns_b] = total[0]
            out_ref[view, pl.ds(SUB, SUB), columns_b] = total[1]
            return 0

        lax.fori_loop(0, blocks, compose, 0)

    for view in range(2):
        at = send.at[view, :, pl.ds(0, n_depth - 1)]
        pltpu.make_async_copy(at, at, a2a_send.at[view]).wait()

    @pl.when(area < n_area - 1)
    def _():
        for b in range(blocks):
            pltpu.make_async_copy(own.at[b], own.at[b], shear_send.at[b]).wait()
        pltpu.make_async_copy(edge_out.at[1], edge_out.at[1], halo_send.at[3]).wait()

    @pl.when(area > 0)
    def _():
        pltpu.make_async_copy(edge_out.at[0], edge_out.at[0], halo_send.at[2]).wait()

    @pl.when(depth < n_depth - 1)
    def _():
        at = F.at[pl.ds(1, blocks), 0, pl.ds(SUB, rows)]
        pltpu.make_async_copy(at, at, halo_send.at[0]).wait()

    @pl.when(depth > 0)
    def _():
        at = F.at[pl.ds(1, blocks), planes + 1, pl.ds(SUB, rows)]
        pltpu.make_async_copy(at, at, halo_send.at[1]).wait()


def solution(mesh):
    n_area, n_depth = mesh.shape["area"], mesh.shape["depth"]

    def shards(field, materials, tf_table, view_order, shear_offset):
        planes, rows, columns = field.shape
        blocks = columns // LANES
        part = rows // n_depth
        f32 = jnp.float32
        image = pl.pallas_call(
            functools.partial(kernel, n_area, n_depth),
            out_shape=jax.ShapeDtypeStruct((2, 4 * part, columns), f32),
            in_specs=[pl.BlockSpec(memory_space=pl.ANY)] * 5,
            out_specs=pl.BlockSpec(memory_space=pltpu.VMEM),
            scratch_shapes=[
                pltpu.VMEM((blocks + 2, planes + 2, rows + 2 * SUB, LANES), f32),
                pltpu.VMEM((blocks, planes, rows, LANES), jnp.int32),
                pltpu.SMEM(tf_table.shape, f32),
                pltpu.SMEM(view_order.shape, jnp.int32),
                pltpu.SMEM(shear_offset.shape, jnp.int32),
                pltpu.VMEM((2, blocks, planes, LANES), f32),
                pltpu.VMEM((2, blocks, planes, LANES), f32),
                pltpu.VMEM((blocks, 7, rows, LANES), f32),
                pltpu.VMEM((blocks, 4, rows, LANES), f32),
                pltpu.VMEM((blocks, 4, rows, LANES), f32),
                pltpu.VMEM((4, 2 * rows, LANES), f32),
                pltpu.VMEM((2, blocks, n_depth, 4 * part, LANES), f32),
                pltpu.VMEM((2, blocks, n_depth, 4 * part, LANES), f32),
                pltpu.SemaphoreType.DMA((2 * blocks,)),
                pltpu.SemaphoreType.DMA((3,)),
                pltpu.SemaphoreType.DMA((4,)),
                pltpu.SemaphoreType.DMA((4,)),
                pltpu.SemaphoreType.DMA((blocks,)),
                pltpu.SemaphoreType.DMA((blocks,)),
                pltpu.SemaphoreType.DMA((2,)),
                pltpu.SemaphoreType.DMA((2,)),
            ],
            compiler_params=pltpu.CompilerParams(
                collective_id=0, has_side_effects=True, vmem_limit_bytes=48 * 2**20
            ),
            name="render",
        )(field, materials, tf_table, view_order, shear_offset)
        return image.reshape(2, 4, part, columns)

    in_specs = (P("depth", "area", None), P("depth", "area", None), P(), P(), P())
    out_specs = P(None, None, ("area", "depth"), None)
    return jax.shard_map(shards, mesh=mesh, in_specs=in_specs, out_specs=out_specs, check_vma=False)
```

profile of v0, /device:TPU:0, one launch (start us, length us, event | category | flops | bytes accessed | tf_op | source)
XLA Modules:
  0.0 33.5 jit_solution(4164374324968318712)
XLA Ops:
  0.0 0.0 copy-start
  0.0 2.2 %copy-done = f32[32,64,512]{2,1,0:T(8,128)S(1)} copy-done((f32[32,64,512]{2,1,0:T(8,128)S(1)}, f32[32,64,512]{2,1,0:T(8,128)}, u32[]{:S(2)}) %copy-start) | copy-done | bytes 4194328
  2.2 0.0 copy-start.1
  2.2 0.7 %copy-done.1 = f32[4,16]{1,0:T(4,128)S(1)} copy-done((f32[4,16]{1,0:T(4,128)S(1)}, f32[4,16]{1,0:T(4,128)}, u32[]{:S(2)}) %copy-start.1) | copy-done | bytes 280
  2.9 0.0 copy-start.2
  2.9 0.7 %copy-done.2 = s32[2,16]{1,0:T(2,128)S(1)} copy-done((s32[2,16]{1,0:T(2,128)S(1)}, s32[2,16]{1,0:T(2,128)}, u32[]{:S(2)}) %copy-start.2) | copy-done | bytes 152
  3.6 0.0 copy-start.3
  3.6 0.7 %copy-done.3 = s32[16]{0:T(128)S(1)} copy-done((s32[16]{0:T(128)S(1)}, s32[16]{0:T(128)}, u32[]{:S(2)}) %copy-start.3) | copy-done | bytes 88
  4.2 28.7 %render.1 = f32[2,16,512]{2,1,0:T(8,128)S(1)} custom-call(f32[32,64,512]{2,1,0:T(8,128)S(1)} %copy-done, s32[32,64,512]{2,1,0:T(8,128)} %mat_hbm.1, f32[4,16]{1,0:T(4,128)S(1)} %copy-done.1, s32[2,16]{1,0:T(2,128)S(1)} %copy-done.2, s32[16]{0:T(128)S(1)} %copy-done.3), custom_call_target="tpu_custom_call" | custom-call | tf_op jit(solution)/shard_map/render/pallas_call | solution.py:450
  32.9 0.7 %reshape.3 = f32[2,4,4,512]{3,2,1,0:T(4,128)} reshape(f32[2,16,512]{2,1,0:T(8,128)S(1)} %render.1) | data formatting | bytes 131072 | tf_op jit(solution)/shard_map/reshape | solution.py:483
Async XLA Ops:
  0.0 2.2 %copy-start = (f32[32,64,512]{2,1,0:T(8,128)S(1)}, f32[32,64,512]{2,1,0:T(8,128)}, u32[]{:S(2)}) copy-start(f32[32,64,512]{2,1,0:T(8,128)} %field_hbm.1) | copy-start | bytes 12582916
  2.2 0.7 %copy-start.1 = (f32[4,16]{1,0:T(4,128)S(1)}, f32[4,16]{1,0:T(4,128)}, u32[]{:S(2)}) copy-start(f32[4,16]{1,0:T(4,128)} %tf_hbm.1) | copy-start | bytes 772
  2.9 0.7 %copy-start.2 = (s32[2,16]{1,0:T(2,128)S(1)}, s32[2,16]{1,0:T(2,128)}, u32[]{:S(2)}) copy-start(s32[2,16]{1,0:T(2,128)} %order_hbm.1) | copy-start | bytes 388
  3.6 0.7 %copy-start.3 = (s32[16]{0:T(128)S(1)}, s32[16]{0:T(128)}, u32[]{:S(2)}) copy-start(s32[16]{0:T(128)} %shear_hbm.1) | copy-start | bytes 196
where the time goes:
time: 33.9 us; the launch traced here: 33.5 us
  Pallas kernels  28.7 us (85%)
  local copies, waits for them, and re-layouts  4.85 us (14%)
    pallas_call x1, Pallas kernels, shards(): pl.pallas_call(functools.partial(kernel, n_area, n_depth), out_shape=jax....  28.7 us
    unnamed x8, local copies, waits for them, and re-layouts  4.2 us

commit v1 on v0

--- a/solution.py
+++ b/solution.py
@@ -50,8 +50,10 @@
     recv,
     load_sem,
     small_sem,
-    halo_send,
-    halo_recv,
+    plane_send,
+    plane_recv,
+    edge_send,
+    edge_recv,
     shear_send,
     shear_recv,
     a2a_send,
@@ -61,6 +63,7 @@
     blocks = columns // LANES
     tiles = rows // SUB
     part = rows // n_depth
+    halves = SUB // part
     area, depth = lax.axis_index("area"), lax.axis_index("depth")
     zero = jnp.zeros((SUB, LANES), jnp.float32)
 
@@ -123,6 +126,13 @@
             for r in range(tiles):
                 F[b + 1, at, pl.ds(SUB + r * SUB, SUB), :] = zero
 
+    for side, outer in ((0, area == 0), (1, area == n_area - 1)):
+
+        @pl.when(outer)
+        def _():
+            for b in range(blocks):
+                edge_in[side, b] = jnp.zeros((planes, LANES), jnp.float32)
+
     @pl.when(depth == 0)
     def _():
         clear_plane(0)
@@ -131,57 +141,13 @@
     def _():
         clear_plane(planes + 1)
 
-    @pl.when(jnp.logical_and(area > 0, area < n_area - 1))
-    def _():
-        pl.semaphore_wait(barrier, n_depth - 1 + 2)
-
-    @pl.when(jnp.logical_or(area == 0, area == n_area - 1))
-    def _():
-        pl.semaphore_wait(barrier, n_depth - 1 + 1)
-
-    def plane_copy(b, src, dst, slot, peer):
-        return pltpu.make_async_remote_copy(
-            src_ref=field_hbm.at[src, :, pl.ds(b * LANES, LANES)],
-            dst_ref=F.at[b + 1, dst, pl.ds(SUB, rows)],
-            send_sem=halo_send.at[slot],
-            recv_sem=halo_recv.at[slot],
-            device_id={"depth": peer},
-            device_id_type=MESH,
-        )
-
-    @pl.when(depth < n_depth - 1)
-    def _():
+    def pack_edges():
         for b in range(blocks):
-            plane_copy(b, planes - 1, 0, 0, depth + 1).start()
-
-    @pl.when(depth > 0)
-    def _():
+            wait_field(b)
         for b in range(blocks):
-            plane_copy(b, 0, planes + 1, 1, depth - 1).start()
-
-    for b in range(blocks):
-        wait_field(b)
-        for k in range(planes):
-            edge_out[0, b, pl.ds(k, 1), :] = F[b + 1, k + 1, pl.ds(SUB, 1), :]
-            edge_out[1, b, pl.ds(k, 1), :] = F[b + 1, k + 1, pl.ds(SUB + rows - 1, 1), :]
-
-    def edge_copy(src, peer):
-        return pltpu.make_async_remote_copy(
-            src_ref=edge_out.at[src],
-            dst_ref=edge_in.at[1 - src],
-            send_sem=halo_send.at[2 + src],
-            recv_sem=halo_recv.at[2 + src],
-            device_id={"area": peer},
-            device_id_type=MESH,
-        )
-
-    @pl.when(area < n_area - 1)
-    def _():
-        edge_copy(1, area + 1).start()
-
-    @pl.when(area > 0)
-    def _():
-        edge_copy(0, area - 1).start()
+            for k in range(planes):
+                edge_out[0, b, pl.ds(k, 1), :] = F[b + 1, k + 1, pl.ds(SUB, 1), :]
+                edge_out[1, b, pl.ds(k, 1), :] = F[b + 1, k + 1, pl.ds(SUB + rows - 1, 1), :]
 
     for copy in small:
         copy.wait()
@@ -190,13 +156,13 @@
     is_first, is_last = lane_id == 0, lane_id == LANES - 1
     table = []
     for channel in range(4):
-        halves = []
+        pair = []
         for half in range(2):
             values = jnp.full((SUB, LANES), tf_s[channel, half * SUB], jnp.float32)
             for entry in range(1, SUB):
                 values = jnp.where(sub_id == entry, tf_s[channel, half * SUB + entry], values)
-            halves.append(values)
-        table.append(halves)
+            pair.append(values)
+        table.append(pair)
 
     def cells(b, k, row):
         mid = pl.ds(pl.multiple_of(row + SUB, SUB), SUB)
@@ -218,18 +184,59 @@
         a = looked[3] * (1.0 - jnp.exp2(EXP_SCALE * (c * c + gm2)))
         return looked[:3], shade * a, 1.0 - a
 
-    def interior(b, tile):
+    def march(b, tile, first, last):
         row = tile * SUB
         through = zero + 1.0
         front, back = [zero] * 3, [zero] * 3
-        for k in range(1, planes - 1):
+        for k in range(first, last):
             colour, sa, keep = cells(b, k, row)
             weight = through * sa
             front = [f + t * weight for f, t in zip(front, colour)]
             back = [f * keep + t * sa for f, t in zip(back, colour)]
             through = through * keep
+        return through, front, back
+
+    def interior(b, tile):
+        at = pl.ds(pl.multiple_of(tile * SUB, SUB), SUB)
+        through, front, back = march(b, tile, 1, planes - 1)
         for i, value in enumerate([through, *front, *back]):
-            state[b, i, pl.ds(pl.multiple_of(row, SUB), SUB), :] = value
+            state[b, i, at, :] = value
+
+    def emit(b, tile, front, back, through):
+        at = pl.ds(pl.multiple_of(tile * SUB, SUB), SUB)
+        opacity = 1.0 - through
+        for i, (first, second) in enumerate(zip([*front, opacity], [*back, opacity])):
+            own[b, i, at, :] = second
+            for half in range(halves):
+                send[0, b, tile * halves + half, pl.ds(i * part, part), :] = first[
+                    half * part : (half + 1) * part
+                ]
+
+        @pl.when(area < n_area - 1)
+        def _():
+            pltpu.make_async_remote_copy(
+                src_ref=own.at[b, :, at],
+                dst_ref=near.at[b, :, at],
+                send_sem=shear_send.at[b],
+                recv_sem=shear_recv.at[b],
+                device_id={"area": area + 1},
+                device_id_type=MESH,
+            ).start()
+
+        for half in range(halves):
+            peer = tile * halves + half
+
+            @pl.when(peer != depth)
+            def _():
+                part_copy(0, b, peer).start()
+
+            @pl.when(peer == depth)
+            def _():
+                recv[0, b, depth] = send[0, b, depth]
+
+    def full(b, tile):
+        through, front, back = march(b, tile, 0, planes)
+        emit(b, tile, front, back, through)
 
     def ends(b, tile):
         row = tile * SUB
@@ -237,43 +244,20 @@
         colour0, sa0, keep0 = cells(b, 0, row)
         colour1, sa1, keep1 = cells(b, planes - 1, row)
         through = state[b, 0, at, :]
-        opacity = 1.0 - through * keep0 * keep1
-        for i in range(4):
-            if i == 3:
-                first, second = opacity, opacity
-            else:
-                c0, c1 = colour0[i] * sa0, colour1[i] * sa1
-                first = c0 + keep0 * (state[b, 1 + i, at, :] + through * c1)
-                second = c1 + keep1 * (state[b, 4 + i, at, :] + through * c0)
-            own[b, i, at, :] = second
-            for half in range(SUB // part):
-                send[0, b, tile * (SUB // part) + half, pl.ds(i * part, part), :] = first[
-                    half * part : (half + 1) * part
-                ]
-
-    def send_view(view, b):
-        def one(i, _):
-            peer = lax.rem(depth + i, n_depth)
-            pltpu.make_async_remote_copy(
-                src_ref=send.at[view, b, peer],
-                dst_ref=recv.at[view, b, depth],
-                send_sem=a2a_send.at[view],
-                recv_sem=a2a_recv.at[view],
-                device_id={"depth": peer},
-                device_id_type=MESH,
-            ).start()
-            return 0
-
-        lax.fori_loop(1, n_depth, one, 0)
-        recv[view, b, depth] = send[view, b, depth]
-
-    def shear_copy(b):
+        front, back = [], []
+        for i in range(3):
+            c0, c1 = colour0[i] * sa0, colour1[i] * sa1
+            front.append(c0 + keep0 * (state[b, 1 + i, at, :] + through * c1))
+            back.append(c1 + keep1 * (state[b, 4 + i, at, :] + through * c0))
+        emit(b, tile, front, back, through * keep0 * keep1)
+
+    def part_copy(view, b, peer):
         return pltpu.make_async_remote_copy(
-            src_ref=own.at[b],
-            dst_ref=near.at[b],
-            send_sem=shear_send.at[b],
-            recv_sem=shear_recv.at[b],
-            device_id={"area": area + 1},
+            src_ref=send.at[view, b, peer],
+            dst_ref=recv.at[view, b, depth],
+            send_sem=a2a_send.at[view],
+            recv_sem=a2a_recv.at[view],
+            device_id={"depth": peer},
             device_id_type=MESH,
         )
 
@@ -291,95 +275,136 @@
         for tile in range(tiles):
             for i in range(4):
                 moved = window[i, pl.ds(rows + tile * SUB - offset, SUB), :]
-                for half in range(SUB // part):
-                    send[1, b, tile * (SUB // part) + half, pl.ds(i * part, part), :] = moved[
+                for half in range(halves):
+                    send[1, b, tile * halves + half, pl.ds(i * part, part), :] = moved[
                         half * part : (half + 1) * part
                     ]
-        send_view(1, b)
-
-    @pl.when(area == 0)
-    def _():
-        for i in range(4):
+
+        def one(i, _):
+            part_copy(1, b, lax.rem(depth + i, n_depth)).start()
+            return 0
+
+        lax.fori_loop(1, n_depth, one, 0)
+        recv[1, b, depth] = send[1, b, depth]
+
+    inner = tiles - 2
+    ahead, early = depth * 0, 2
+
+    def early_tile(i, _):
+        b = i // inner
+        tile = 1 + i % inner
+
+        @pl.when(tile == 1)
+        def _():
+            wait_mat(b)
+
+        interior(b, tile)
+        return 0
+
+    @pl.when(ahead > 0)
+    def _():
+        pack_edges()
+        lax.fori_loop(0, ahead, early_tile, 0)
+
+    @pl.when(jnp.logical_and(area > 0, area < n_area - 1))
+    def _():
+        pl.semaphore_wait(barrier, n_depth - 1 + 2)
+
+    @pl.when(jnp.logical_or(area == 0, area == n_area - 1))
+    def _():
+        pl.semaphore_wait(barrier, n_depth - 1 + 1)
+
+    def plane_copy(b, src, dst, way, peer):
+        return pltpu.make_async_remote_copy(
+            src_ref=field_hbm.at[src, :, pl.ds(b * LANES, LANES)],
+            dst_ref=F.at[b + 1, dst, pl.ds(SUB, rows)],
+            send_sem=plane_send.at[way],
+            recv_sem=plane_recv.at[way, b],
+            device_id={"depth": peer},
+            device_id_type=MESH,
+        )
+
+    for b in range(blocks):
+
+        @pl.when(depth < n_depth - 1)
+        def _():
+            plane_copy(b, planes - 1, 0, 0, depth + 1).start()
+
+        @pl.when(depth > 0)
+        def _():
+            plane_copy(b, 0, planes + 1, 1, depth - 1).start()
+
+    @pl.when(ahead == 0)
+    def _():
+        pack_edges()
+
+    def edge_copy(side, peer):
+        return pltpu.make_async_remote_copy(
+            src_ref=edge_out.at[side],
+            dst_ref=edge_in.at[1 - side],
+            send_sem=edge_send.at[side],
+            recv_sem=edge_recv.at[1 - side],
+            device_id={"area": peer},
+            device_id_type=MESH,
+        )
+
+    @pl.when(area < n_area - 1)
+    def _():
+        edge_copy(1, area + 1).start()
+
+    @pl.when(area > 0)
+    def _():
+        edge_copy(0, area - 1).start()
+
+    for i in range(4):
+
+        @pl.when(area == 0)
+        def _():
             for tile in range(tiles):
                 window[i, pl.ds(tile * SUB, SUB), :] = zero
 
-    inner = tiles - 2
-    early = 2
-
-    def first_pass(i, _):
-        b = i // inner
-        tile = 1 + i % inner
-
-        @pl.when(tile == 1)
-        def _():
-            wait_mat(b)
-
-        interior(b, tile)
-        return 0
-
-    lax.fori_loop(0, early * inner, first_pass, 0)
-
-    @pl.when(depth > 0)
-    def _():
-        at = F.at[pl.ds(1, blocks), 0, pl.ds(SUB, rows)]
-        pltpu.make_async_copy(at, at, halo_recv.at[0]).wait()
-
-    @pl.when(depth < n_depth - 1)
-    def _():
-        at = F.at[pl.ds(1, blocks), planes + 1, pl.ds(SUB, rows)]
-        pltpu.make_async_copy(at, at, halo_recv.at[1]).wait()
-
-    @pl.when(area > 0)
-    def _():
-        pltpu.make_async_copy(edge_in.at[0], edge_in.at[0], halo_recv.at[3]).wait()
+    lax.fori_loop(ahead, inner * early, early_tile, 0)
+
+    for side, outer, at_row in ((0, area == 0, SUB - 1), (1, area == n_area - 1, SUB + rows)):
+
+        @pl.when(jnp.logical_not(outer))
+        def _():
+            pltpu.make_async_copy(edge_in.at[side], edge_in.at[side], edge_recv.at[side]).wait()
+
         for b in range(blocks):
             for k in range(planes):
-                F[b + 1, k + 1, pl.ds(SUB - 1, 1), :] = edge_in[0, b, pl.ds(k, 1), :]
-
-    @pl.when(area < n_area - 1)
-    def _():
-        pltpu.make_async_copy(edge_in.at[1], edge_in.at[1], halo_recv.at[2]).wait()
-        for b in range(blocks):
-            for k in range(planes):
-                F[b + 1, k + 1, pl.ds(SUB + rows, 1), :] = edge_in[1, b, pl.ds(k, 1), :]
-
-    @pl.when(area == 0)
-    def _():
-        for b in range(blocks):
-            for k in range(planes):
-                F[b + 1, k + 1, pl.ds(SUB - 1, 1), :] = zero[:1]
-
-    @pl.when(area == n_area - 1)
-    def _():
-        for b in range(blocks):
-            for k in range(planes):
-                F[b + 1, k + 1, pl.ds(SUB + rows, 1), :] = zero[:1]
+                value = edge_in[side, b, pl.ds(k, 1), :]
+                F[b + 1, k + 1, pl.ds(at_row, 1), :] = value
 
     def block(b, _):
-        late = b // early
+        late = jnp.where(b >= early, 1, 0)
+
+        @pl.when(depth > 0)
+        def _():
+            at = F.at[b + 1, 0, pl.ds(SUB, rows)]
+            pltpu.make_async_copy(at, at, plane_recv.at[0, b]).wait()
+
+        @pl.when(depth < n_depth - 1)
+        def _():
+            at = F.at[b + 1, planes + 1, pl.ds(SUB, rows)]
+            pltpu.make_async_copy(at, at, plane_recv.at[1, b]).wait()
 
         @pl.when(b >= early)
         def _():
             wait_mat(b)
 
         def rest(t, _):
-            interior(b, t * ((tiles - 1) - (tiles - 2) * late))
+            full(b, t * ((tiles - 1) - (tiles - 2) * late))
             return 0
 
         lax.fori_loop(0, 2 + inner * late, rest, 0)
 
         def finish(t, _):
-            ends(b, 2 * t)
-            ends(b, 2 * t + 1)
+            ends(b, 1 + 2 * t)
+            ends(b, 2 + 2 * t)
             return 0
 
-        lax.fori_loop(0, tiles // 2, finish, 0)
-
-        @pl.when(area < n_area - 1)
-        def _():
-            shear_copy(b).start()
-
-        send_view(0, b)
+        lax.fori_loop(0, (inner // 2) * (1 - late), finish, 0)
 
         @pl.when(b > 0)
         def _():
@@ -422,21 +447,21 @@
     def _():
         for b in range(blocks):
             pltpu.make_async_copy(own.at[b], own.at[b], shear_send.at[b]).wait()
-        pltpu.make_async_copy(edge_out.at[1], edge_out.at[1], halo_send.at[3]).wait()
+        pltpu.make_async_copy(edge_out.at[1], edge_out.at[1], edge_send.at[1]).wait()
 
     @pl.when(area > 0)
     def _():
-        pltpu.make_async_copy(edge_out.at[0], edge_out.at[0], halo_send.at[2]).wait()
+        pltpu.make_async_copy(edge_out.at[0], edge_out.at[0], edge_send.at[0]).wait()
 
     @pl.when(depth < n_depth - 1)
     def _():
         at = F.at[pl.ds(1, blocks), 0, pl.ds(SUB, rows)]
-        pltpu.make_async_copy(at, at, halo_send.at[0]).wait()
+        pltpu.make_async_copy(at, at, plane_send.at[0]).wait()
 
     @pl.when(depth > 0)
     def _():
         at = F.at[pl.ds(1, blocks), planes + 1, pl.ds(SUB, rows)]
-        pltpu.make_async_copy(at, at, halo_send.at[1]).wait()
+        pltpu.make_async_copy(at, at, plane_send.at[1]).wait()
 
 
 def solution(mesh):
@@ -450,7 +475,7 @@
         image = pl.pallas_call(
             functools.partial(kernel, n_area, n_depth),
             out_shape=jax.ShapeDtypeStruct((2, 4 * part, columns), f32),
-            in_specs=[pl.BlockSpec(memory_space=pl.ANY)] * 5,
+            in_specs=[pl.BlockSpec(memory_space=pltpu.HBM)] * 5,
             out_specs=pl.BlockSpec(memory_space=pltpu.VMEM),
             scratch_shapes=[
                 pltpu.VMEM((blocks + 2, planes + 2, rows + 2 * SUB, LANES), f32),
@@ -468,15 +493,17 @@
                 pltpu.VMEM((2, blocks, n_depth, 4 * part, LANES), f32),
                 pltpu.SemaphoreType.DMA((2 * blocks,)),
                 pltpu.SemaphoreType.DMA((3,)),
-                pltpu.SemaphoreType.DMA((4,)),
-                pltpu.SemaphoreType.DMA((4,)),
+                pltpu.SemaphoreType.DMA((2,)),
+                pltpu.SemaphoreType.DMA((2, blocks)),
+                pltpu.SemaphoreType.DMA((2,)),
+                pltpu.SemaphoreType.DMA((2,)),
                 pltpu.SemaphoreType.DMA((blocks,)),
                 pltpu.SemaphoreType.DMA((blocks,)),
                 pltpu.SemaphoreType.DMA((2,)),
                 pltpu.SemaphoreType.DMA((2,)),
             ],
             compiler_params=pltpu.CompilerParams(
-                collective_id=0, has_side_effects=True, vmem_limit_bytes=48 * 2**20
+                collective_id=0, has_side_effects=True, vmem_limit_bytes=60 * 2**20
             ),
             name="render",
         )(field, materials, tf_table, view_order, shear_offset)

time: 33.9 us -> 29 us (0.86)
  local copies, waits for them, and re-layouts: 4.85 us -> 1.49 us
  Pallas kernels: 28.7 us -> 27.1 us
    unnamed x8 -> x0, local copies, waits for them, and re-layouts: 4.2 us -> none
    pallas_call x1, Pallas kernels: 28.7 us -> 27.1 us  [shards(): pl.pallas_call(functools.partial(kernel, n_area, n_depth), out_shape=jax....]
    reshape x1, local copies, waits for them, and re-layouts: 0.65 us -> 1.49 us  [shards(): return image.reshape(2, 4, part, columns)]
where the time goes in v1:
time: 29 us; the launch traced here: 28.6 us
  Pallas kernels  27.1 us (93%)
  local copies, waits for them, and re-layouts  1.49 us (5%)
    pallas_call x1, Pallas kernels, shards(): pl.pallas_call(functools.partial(kernel, n_area, n_depth), out_shape=jax....  27.1 us
    reshape x1, local copies, waits for them, and re-layouts, shards(): return image.reshape(2, 4, part, columns)  1.49 us

profile of v1, /device:TPU:0, one launch (start us, length us, event | category | flops | bytes accessed | tf_op | source)
XLA Modules:
  0.0 28.6 jit_solution(2332231930892742986)
XLA Ops:
  0.0 27.1 %render.1 = f32[2,16,512]{2,1,0:T(8,128)} custom-call(f32[32,64,512]{2,1,0:T(8,128)} %field_hbm.1, s32[32,64,512]{2,1,0:T(8,128)} %mat_hbm.1, f32[4,16]{1,0:T(4,128)} %tf_hbm.1, s32[2,16]{1,0:T(2,128)} %order_hbm.1, s32[16]{0:T(128)} %shear_hbm.1), custom_call_target="tpu_custom_call" | custom-call | tf_op jit(solution)/shard_map/render/pallas_call | solution.py:475
  27.1 1.5 %reshape.3 = f32[2,4,4,512]{3,2,1,0:T(4,128)} reshape(f32[2,16,512]{2,1,0:T(8,128)} %render.1) | data formatting | bytes 131072 | tf_op jit(solution)/shard_map/reshape | solution.py:510

commit v2 on v1

--- a/solution.py
+++ b/solution.py
@@ -13,13 +13,13 @@
 EXP_SCALE = -0.25 * 1.4426950408889634
 
 
-def sublane_gather(table, index):
+def gather(table, index, axis):
     dims = lax.GatherDimensionNumbers(
         offset_dims=(),
-        collapsed_slice_dims=(0,),
-        start_index_map=(0,),
-        operand_batching_dims=(1,),
-        start_indices_batching_dims=(1,),
+        collapsed_slice_dims=(axis,),
+        start_index_map=(axis,),
+        operand_batching_dims=(1 - axis,),
+        start_indices_batching_dims=(1 - axis,),
     )
     return lax.gather(
         table, index[..., None], dims, (1, 1), mode=lax.GatherScatterMode.PROMISE_IN_BOUNDS
@@ -48,6 +48,7 @@
     window,
     send,
     recv,
+    final,
     load_sem,
     small_sem,
     plane_send,
@@ -64,16 +65,21 @@
     tiles = rows // SUB
     part = rows // n_depth
     halves = SUB // part
+    last = blocks - 1
     area, depth = lax.axis_index("area"), lax.axis_index("depth")
     zero = jnp.zeros((SUB, LANES), jnp.float32)
 
-    for b in range(blocks):
+    def load_field(b):
         pltpu.make_async_copy(
             field_hbm.at[:, :, pl.ds(b * LANES, LANES)],
             F.at[b + 1, pl.ds(1, planes), pl.ds(SUB, rows)],
             load_sem.at[b],
         ).start()
+
+    load_field(0)
     for b in range(blocks):
+        if b + 1 < blocks:
+            load_field(b + 1)
         pltpu.make_async_copy(
             mat_hbm.at[:, :, pl.ds(b * LANES, LANES)], M.at[b], load_sem.at[blocks + b]
         ).start()
@@ -141,13 +147,10 @@
     def _():
         clear_plane(planes + 1)
 
-    def pack_edges():
-        for b in range(blocks):
-            wait_field(b)
-        for b in range(blocks):
-            for k in range(planes):
-                edge_out[0, b, pl.ds(k, 1), :] = F[b + 1, k + 1, pl.ds(SUB, 1), :]
-                edge_out[1, b, pl.ds(k, 1), :] = F[b + 1, k + 1, pl.ds(SUB + rows - 1, 1), :]
+    def pack_edges(b):
+        for k in range(planes):
+            edge_out[0, b, pl.ds(k, 1), :] = F[b + 1, k + 1, pl.ds(SUB, 1), :]
+            edge_out[1, b, pl.ds(k, 1), :] = F[b + 1, k + 1, pl.ds(SUB + rows - 1, 1), :]
 
     for copy in small:
         copy.wait()
@@ -155,7 +158,7 @@
     lane_id = lax.broadcasted_iota(jnp.int32, (SUB, LANES), 1)
     is_first, is_last = lane_id == 0, lane_id == LANES - 1
     table = []
-    for channel in range(4):
+    for channel in range(3):
         pair = []
         for half in range(2):
             values = jnp.full((SUB, LANES), tf_s[channel, half * SUB], jnp.float32)
@@ -163,6 +166,9 @@
                 values = jnp.where(sub_id == entry, tf_s[channel, half * SUB + entry], values)
             pair.append(values)
         table.append(pair)
+    opacities = jnp.zeros((SUB, LANES), jnp.float32)
+    for entry in range(tf_s.shape[1]):
+        opacities = jnp.where(lane_id == entry, tf_s[3, entry], opacities)
 
     def cells(b, k, row):
         mid = pl.ds(pl.multiple_of(row + SUB, SUB), SUB)
@@ -178,11 +184,11 @@
         m = M[b, k, pl.ds(pl.multiple_of(row, SUB), SUB), :]
         upper, index = m > SUB - 1, m & (SUB - 1)
         looked = [
-            jnp.where(upper, sublane_gather(hi, index), sublane_gather(lo, index))
+            jnp.where(upper, gather(hi, index, 0), gather(lo, index, 0))
             for lo, hi in table
         ]
-        a = looked[3] * (1.0 - jnp.exp2(EXP_SCALE * (c * c + gm2)))
-        return looked[:3], shade * a, 1.0 - a
+        a = gather(opacities, m, 1) * (1.0 - jnp.exp2(EXP_SCALE * (c * c + gm2)))
+        return looked, shade * a, 1.0 - a
 
     def march(b, tile, first, last):
         row = tile * SUB
@@ -190,9 +196,9 @@
         front, back = [zero] * 3, [zero] * 3
         for k in range(first, last):
             colour, sa, keep = cells(b, k, row)
-            weight = through * sa
-            front = [f + t * weight for f, t in zip(front, colour)]
-            back = [f * keep + t * sa for f, t in zip(back, colour)]
+            colour = [t * sa for t in colour]
+            front = [f + c * through for f, c in zip(front, colour)]
+            back = [f * keep + c for f, c in zip(back, colour)]
             through = through * keep
         return through, front, back
 
@@ -263,7 +269,16 @@
 
     offset = shear_s[depth]
 
-    def shear(b):
+    edge = int(n_depth**0.5)
+    far = sorted(
+        ((x, z) for x in range(edge) for z in range(edge) if x or z),
+        key=lambda p: -min(p[0], edge - p[0]) - min(p[1], edge - p[1]),
+    )
+
+    def peer_at(x, z):
+        return lax.rem(depth // edge + x, edge) * edge + lax.rem(depth + z, edge)
+
+    def shear(b, place, slot, sems):
         @pl.when(area > 0)
         def _():
             pltpu.make_async_copy(near.at[b], near.at[b], shear_recv.at[b]).wait()
@@ -280,39 +295,20 @@
                         half * part : (half + 1) * part
                     ]
 
-        def one(i, _):
-            part_copy(1, b, lax.rem(depth + i, n_depth)).start()
-            return 0
-
-        lax.fori_loop(1, n_depth, one, 0)
-        recv[1, b, depth] = send[1, b, depth]
+        for x, z in far:
+            peer = peer_at(x, z)
+            pltpu.make_async_remote_copy(
+                src_ref=send.at[1, b, peer],
+                dst_ref=place.at[slot[0], slot[1], depth],
+                send_sem=a2a_send.at[1],
+                recv_sem=sems,
+                device_id={"depth": peer},
+                device_id_type=MESH,
+            ).start()
+        place[slot[0], slot[1], depth] = send[1, b, depth]
 
     inner = tiles - 2
-    ahead, early = depth * 0, 2
-
-    def early_tile(i, _):
-        b = i // inner
-        tile = 1 + i % inner
-
-        @pl.when(tile == 1)
-        def _():
-            wait_mat(b)
-
-        interior(b, tile)
-        return 0
-
-    @pl.when(ahead > 0)
-    def _():
-        pack_edges()
-        lax.fori_loop(0, ahead, early_tile, 0)
-
-    @pl.when(jnp.logical_and(area > 0, area < n_area - 1))
-    def _():
-        pl.semaphore_wait(barrier, n_depth - 1 + 2)
-
-    @pl.when(jnp.logical_or(area == 0, area == n_area - 1))
-    def _():
-        pl.semaphore_wait(barrier, n_depth - 1 + 1)
+    early = 2
 
     def plane_copy(b, src, dst, way, peer):
         return pltpu.make_async_remote_copy(
@@ -324,8 +320,7 @@
             device_id_type=MESH,
         )
 
-    for b in range(blocks):
-
+    def send_planes(b):
         @pl.when(depth < n_depth - 1)
         def _():
             plane_copy(b, planes - 1, 0, 0, depth + 1).start()
@@ -334,50 +329,85 @@
         def _():
             plane_copy(b, 0, planes + 1, 1, depth - 1).start()
 
-    @pl.when(ahead == 0)
-    def _():
-        pack_edges()
-
-    def edge_copy(side, peer):
+    def edge_copy(b, side, peer):
         return pltpu.make_async_remote_copy(
-            src_ref=edge_out.at[side],
-            dst_ref=edge_in.at[1 - side],
+            src_ref=edge_out.at[side, b],
+            dst_ref=edge_in.at[1 - side, b],
             send_sem=edge_send.at[side],
-            recv_sem=edge_recv.at[1 - side],
+            recv_sem=edge_recv.at[1 - side, b],
             device_id={"area": peer},
             device_id_type=MESH,
         )
 
-    @pl.when(area < n_area - 1)
-    def _():
-        edge_copy(1, area + 1).start()
-
-    @pl.when(area > 0)
-    def _():
-        edge_copy(0, area - 1).start()
-
-    for i in range(4):
-
-        @pl.when(area == 0)
-        def _():
+    def send_edges(b):
+        pack_edges(b)
+
+        @pl.when(area < n_area - 1)
+        def _():
+            edge_copy(b, 1, area + 1).start()
+
+        @pl.when(area > 0)
+        def _():
+            edge_copy(b, 0, area - 1).start()
+
+    def early_tile(i, _):
+        b = i // inner
+        tile = 1 + i % inner
+
+        @pl.when(tile == 1)
+        def _():
+            wait_mat(b)
+
+        interior(b, tile)
+        return 0
+
+    def early_tile_and_halo(i, _):
+        for b in range(1, blocks):
+
+            @pl.when(i == 2 * b - 1)
+            def _():
+                send_planes(b)
+                if b > 1:
+                    wait_field(b)
+                send_edges(b)
+
+        return early_tile(i, 0)
+
+    @pl.when(jnp.logical_and(area > 0, area < n_area - 1))
+    def _():
+        pl.semaphore_wait(barrier, n_depth - 1 + 2)
+
+    @pl.when(jnp.logical_or(area == 0, area == n_area - 1))
+    def _():
+        pl.semaphore_wait(barrier, n_depth - 1 + 1)
+
+    send_planes(0)
+
+    wait_field(0)
+    wait_field(1)
+    send_edges(0)
+
+    @pl.when(area == 0)
+    def _():
+        for i in range(4):
             for tile in range(tiles):
                 window[i, pl.ds(tile * SUB, SUB), :] = zero
 
-    lax.fori_loop(ahead, inner * early, early_tile, 0)
-
-    for side, outer, at_row in ((0, area == 0, SUB - 1), (1, area == n_area - 1, SUB + rows)):
-
-        @pl.when(jnp.logical_not(outer))
-        def _():
-            pltpu.make_async_copy(edge_in.at[side], edge_in.at[side], edge_recv.at[side]).wait()
-
-        for b in range(blocks):
+    lax.fori_loop(0, inner * early, early_tile_and_halo, 0)
+
+    def block(b, _):
+        late = jnp.where(b >= early, 1, 0)
+
+        for side, outer, at_row in ((0, area == 0, SUB - 1), (1, area == n_area - 1, SUB + rows)):
+
+            @pl.when(jnp.logical_not(outer))
+            def _():
+                at = edge_in.at[side, b]
+                pltpu.make_async_copy(at, at, edge_recv.at[side, b]).wait()
+
             for k in range(planes):
                 value = edge_in[side, b, pl.ds(k, 1), :]
                 F[b + 1, k + 1, pl.ds(at_row, 1), :] = value
-
-    def block(b, _):
-        late = jnp.where(b >= early, 1, 0)
 
         @pl.when(depth > 0)
         def _():
@@ -408,36 +438,57 @@
 
         @pl.when(b > 0)
         def _():
-            shear(b - 1)
+            shear(b - 1, recv, (1, b - 1), a2a_recv.at[1])
 
         return 0
 
     lax.fori_loop(0, blocks, block, 0)
-    shear(blocks - 1)
-
-    for view in range(2):
-        at = recv.at[view, :, pl.ds(0, n_depth - 1)]
+    shear(last, final, (0, 0), a2a_recv.at[2])
+
+    low = sub_id < part
+
+    def compose(view, b, held):
+        through = zero + 1.0
+        total = [zero, zero]
+        for k in range(n_depth):
+            layer = order_s[view, k]
+            one, two = [held[view, b, layer, pl.ds(h * SUB, SUB), :] for h in range(2)]
+            total = [total[0] + through * one, total[1] + through * two]
+            opacity = jnp.where(low, pltpu.roll(two, part, 0), two)
+            through = through * (1.0 - opacity)
+        return total
+
+    def compose_last():
+        through = zero + 1.0
+        total = [zero, zero]
+        for k in range(n_depth):
+            layer = order_s[1, k]
+            one, two = [final[0, 0, layer, pl.ds(h * SUB, SUB), :] for h in range(2)]
+            total = [total[0] + through * one, total[1] + through * two]
+            opacity = jnp.where(low, pltpu.roll(two, part, 0), two)
+            through = through * (1.0 - opacity)
+        return total
+
+    def put(view, b, total):
+        columns_b = pl.ds(pl.multiple_of(b * LANES, LANES), LANES)
+        out_ref[view, pl.ds(0, SUB), columns_b] = total[0]
+        out_ref[view, pl.ds(SUB, SUB), columns_b] = total[1]
+
+    for view, count in ((1, last), (0, blocks)):
+        at = recv.at[view, pl.ds(0, count), pl.ds(0, n_depth - 1)]
         pltpu.make_async_copy(at, at, a2a_recv.at[view]).wait()
 
-    low = sub_id < part
-    for view in range(2):
-
-        def compose(b, _):
-            through = zero + 1.0
-            total = [zero, zero]
-            for k in range(n_depth):
-                layer = order_s[view, k]
-                one = recv[view, b, layer, pl.ds(0, SUB), :]
-                two = recv[view, b, layer, pl.ds(SUB, SUB), :]
-                total = [total[0] + through * one, total[1] + through * two]
-                opacity = jnp.where(low, pltpu.roll(two, part, 0), two)
-                through = through * (1.0 - opacity)
-            columns_b = pl.ds(pl.multiple_of(b * LANES, LANES), LANES)
-            out_ref[view, pl.ds(0, SUB), columns_b] = total[0]
-            out_ref[view, pl.ds(SUB, SUB), columns_b] = total[1]
-            return 0
-
-        lax.fori_loop(0, blocks, compose, 0)
+    def some(b, _):
+        for view in range(2):
+            put(view, b, compose(view, b, recv))
+        return 0
+
+    lax.fori_loop(0, last, some, 0)
+    put(0, last, compose(0, last, recv))
+
+    at = final.at[0, 0, pl.ds(0, n_depth - 1)]
+    pltpu.make_async_copy(at, at, a2a_recv.at[2]).wait()
+    put(1, last, compose_last())
 
     for view in range(2):
         at = send.at[view, :, pl.ds(0, n_depth - 1)]
@@ -491,16 +542,17 @@
                 pltpu.VMEM((4, 2 * rows, LANES), f32),
                 pltpu.VMEM((2, blocks, n_depth, 4 * part, LANES), f32),
                 pltpu.VMEM((2, blocks, n_depth, 4 * part, LANES), f32),
+                pltpu.VMEM((1, 1, n_depth, 4 * part, LANES), f32),
                 pltpu.SemaphoreType.DMA((2 * blocks,)),
                 pltpu.SemaphoreType.DMA((3,)),
                 pltpu.SemaphoreType.DMA((2,)),
                 pltpu.SemaphoreType.DMA((2, blocks)),
                 pltpu.SemaphoreType.DMA((2,)),
-                pltpu.SemaphoreType.DMA((2,)),
+                pltpu.SemaphoreType.DMA((2, blocks)),
                 pltpu.SemaphoreType.DMA((blocks,)),
                 pltpu.SemaphoreType.DMA((blocks,)),
                 pltpu.SemaphoreType.DMA((2,)),
-                pltpu.SemaphoreType.DMA((2,)),
+                pltpu.SemaphoreType.DMA((3,)),
             ],
             compiler_params=pltpu.CompilerParams(
                 collective_id=0, has_side_effects=True, vmem_limit_bytes=60 * 2**20

time: 29 us -> 28.4 us (0.979)
  Pallas kernels: 27.1 us -> 26.7 us
    pallas_call x1, Pallas kernels: 27.1 us -> 26.7 us  [shards(): pl.pallas_call(functools.partial(kernel, n_area, n_depth), out_shape=jax....]
where the time goes in v2:
time: 28.4 us; the launch traced here: 28.2 us
  Pallas kernels  26.7 us (94%)
  local copies, waits for them, and re-layouts  1.49 us (5%)
    pallas_call x1, Pallas kernels, shards(): pl.pallas_call(functools.partial(kernel, n_area, n_depth), out_shape=jax....  26.7 us
    reshape x1, local copies, waits for them, and re-layouts, shards(): return image.reshape(2, 4, part, columns)  1.49 us

profile of v2, /device:TPU:0, one launch (start us, length us, event | category | flops | bytes accessed | tf_op | source)
XLA Modules:
  0.0 28.2 jit_solution(9941440284016471087)
XLA Ops:
  0.0 26.7 %render.1 = f32[2,16,512]{2,1,0:T(8,128)} custom-call(f32[32,64,512]{2,1,0:T(8,128)} %field_hbm.1, s32[32,64,512]{2,1,0:T(8,128)} %mat_hbm.1, f32[4,16]{1,0:T(4,128)} %tf_hbm.1, s32[2,16]{1,0:T(2,128)} %order_hbm.1, s32[16]{0:T(128)} %shear_hbm.1), custom_call_target="tpu_custom_call" | custom-call | tf_op jit(solution)/shard_map/render/pallas_call | solution.py:526
  26.7 1.5 %reshape.3 = f32[2,4,4,512]{3,2,1,0:T(4,128)} reshape(f32[2,16,512]{2,1,0:T(8,128)} %render.1) | data formatting | bytes 131072 | tf_op jit(solution)/shard_map/reshape | solution.py:562

commit v3 on v2

--- a/solution.py
+++ b/solution.py
@@ -10,6 +10,7 @@
 MESH = pl.DeviceIdType.MESH
 LANES = 128
 SUB = 8
+LIGHT = 0.7 * 0.24
 EXP_SCALE = -0.25 * 1.4426950408889634
 
 
@@ -165,7 +166,7 @@
             for entry in range(1, SUB):
                 values = jnp.where(sub_id == entry, tf_s[channel, half * SUB + entry], values)
             pair.append(values)
-        table.append(pair)
+        table.append([LIGHT * values for values in pair])
     opacities = jnp.zeros((SUB, LANES), jnp.float32)
     for entry in range(tf_s.shape[1]):
         opacities = jnp.where(lane_id == entry, tf_s[3, entry], opacities)
@@ -179,8 +180,8 @@
         after = pltpu.roll(jnp.where(is_first, F[b + 2, k + 1, mid, :], c), LANES - 1, 1)
         gx = after - before
         gm2 = 0.25 * (gz * gz + gy * gy + gx * gx)
-        lit = jnp.abs(0.168 * gz + 0.21 * gy + 0.224 * gx)
-        shade = 0.3 + lit * lax.rsqrt(gm2 + 1.0)
+        lit = jnp.abs(gz + (0.3 / 0.24) * gy + (0.32 / 0.24) * gx)
+        shade = 0.3 / LIGHT + lit * lax.rsqrt(gm2 + 1.0)
         m = M[b, k, pl.ds(pl.multiple_of(row, SUB), SUB), :]
         upper, index = m > SUB - 1, m & (SUB - 1)
         looked = [
@@ -202,13 +203,14 @@
             through = through * keep
         return through, front, back
 
-    def interior(b, tile):
-        at = pl.ds(pl.multiple_of(tile * SUB, SUB), SUB)
-        through, front, back = march(b, tile, 1, planes - 1)
-        for i, value in enumerate([through, *front, *back]):
-            state[b, i, at, :] = value
-
-    def emit(b, tile, front, back, through):
+    def interior(b, several):
+        marched = [march(b, tile, 1, planes - 1) for tile in several]
+        for tile, (through, front, back) in zip(several, marched):
+            at = pl.ds(pl.multiple_of(tile * SUB, SUB), SUB)
+            for i, value in enumerate([through, *front, *back]):
+                state[b, i, at, :] = value
+
+    def keep(b, tile, front, back, through):
         at = pl.ds(pl.multiple_of(tile * SUB, SUB), SUB)
         opacity = 1.0 - through
         for i, (first, second) in enumerate(zip([*front, opacity], [*back, opacity])):
@@ -218,6 +220,9 @@
                     half * part : (half + 1) * part
                 ]
 
+    def leave(b, tile):
+        at = pl.ds(pl.multiple_of(tile * SUB, SUB), SUB)
+
         @pl.when(area < n_area - 1)
         def _():
             pltpu.make_async_remote_copy(
@@ -240,22 +245,28 @@
             def _():
                 recv[0, b, depth] = send[0, b, depth]
 
-    def full(b, tile):
-        through, front, back = march(b, tile, 0, planes)
-        emit(b, tile, front, back, through)
-
-    def ends(b, tile):
-        row = tile * SUB
-        at = pl.ds(pl.multiple_of(row, SUB), SUB)
-        colour0, sa0, keep0 = cells(b, 0, row)
-        colour1, sa1, keep1 = cells(b, planes - 1, row)
-        through = state[b, 0, at, :]
-        front, back = [], []
-        for i in range(3):
-            c0, c1 = colour0[i] * sa0, colour1[i] * sa1
-            front.append(c0 + keep0 * (state[b, 1 + i, at, :] + through * c1))
-            back.append(c1 + keep1 * (state[b, 4 + i, at, :] + through * c0))
-        emit(b, tile, front, back, through * keep0 * keep1)
+    def full(b, several):
+        marched = [march(b, tile, 0, planes) for tile in several]
+        for tile, (through, front, back) in zip(several, marched):
+            keep(b, tile, front, back, through)
+        for tile in several:
+            leave(b, tile)
+
+    def ends(b, several):
+        for tile in several:
+            row = tile * SUB
+            at = pl.ds(pl.multiple_of(row, SUB), SUB)
+            colour0, sa0, keep0 = cells(b, 0, row)
+            colour1, sa1, keep1 = cells(b, planes - 1, row)
+            through = state[b, 0, at, :]
+            front, back = [], []
+            for i in range(3):
+                c0, c1 = colour0[i] * sa0, colour1[i] * sa1
+                front.append(c0 + keep0 * (state[b, 1 + i, at, :] + through * c1))
+                back.append(c1 + keep1 * (state[b, 4 + i, at, :] + through * c0))
+            keep(b, tile, front, back, through * keep0 * keep1)
+        for tile in several:
+            leave(b, tile)
 
     def part_copy(view, b, peer):
         return pltpu.make_async_remote_copy(
@@ -312,7 +323,7 @@
 
     def plane_copy(b, src, dst, way, peer):
         return pltpu.make_async_remote_copy(
-            src_ref=field_hbm.at[src, :, pl.ds(b * LANES, LANES)],
+            src_ref=F.at[b + 1, src + 1, pl.ds(SUB, rows)],
             dst_ref=F.at[b + 1, dst, pl.ds(SUB, rows)],
             send_sem=plane_send.at[way],
             recv_sem=plane_recv.at[way, b],
@@ -351,24 +362,24 @@
             edge_copy(b, 0, area - 1).start()
 
     def early_tile(i, _):
-        b = i // inner
-        tile = 1 + i % inner
+        b = i // (inner // 3)
+        tile = 1 + 3 * (i % (inner // 3))
 
         @pl.when(tile == 1)
         def _():
             wait_mat(b)
 
-        interior(b, tile)
+        interior(b, [tile + j for j in range(3)])
         return 0
 
     def early_tile_and_halo(i, _):
         for b in range(1, blocks):
 
-            @pl.when(i == 2 * b - 1)
+            @pl.when(i == b - 1)
             def _():
-                send_planes(b)
                 if b > 1:
                     wait_field(b)
+                send_planes(b)
                 send_edges(b)
 
         return early_tile(i, 0)
@@ -381,9 +392,8 @@
     def _():
         pl.semaphore_wait(barrier, n_depth - 1 + 1)
 
+    wait_field(0)
     send_planes(0)
-
-    wait_field(0)
     wait_field(1)
     send_edges(0)
 
@@ -393,7 +403,7 @@
             for tile in range(tiles):
                 window[i, pl.ds(tile * SUB, SUB), :] = zero
 
-    lax.fori_loop(0, inner * early, early_tile_and_halo, 0)
+    lax.fori_loop(0, (inner // 3) * early, early_tile_and_halo, 0)
 
     def block(b, _):
         late = jnp.where(b >= early, 1, 0)
@@ -424,17 +434,16 @@
             wait_mat(b)
 
         def rest(t, _):
-            full(b, t * ((tiles - 1) - (tiles - 2) * late))
+            full(b, [2 * t, 2 * t + 1 + (tiles - 2) * (1 - late)])
             return 0
 
-        lax.fori_loop(0, 2 + inner * late, rest, 0)
+        lax.fori_loop(0, 1 + (tiles // 2 - 1) * late, rest, 0)
 
         def finish(t, _):
-            ends(b, 1 + 2 * t)
-            ends(b, 2 + 2 * t)
+            ends(b, [1 + 3 * t + j for j in range(3)])
             return 0
 
-        lax.fori_loop(0, (inner // 2) * (1 - late), finish, 0)
+        lax.fori_loop(0, (inner // 3) * (1 - late), finish, 0)
 
         @pl.when(b > 0)
         def _():

time: 28.4 us -> 27.8 us (0.979)
  Pallas kernels: 26.7 us -> 26 us
    pallas_call x1, Pallas kernels: 26.7 us -> 26 us  [shards(): pl.pallas_call(functools.partial(kernel, n_area, n_depth), out_shape=jax....]
where the time goes in v3:
time: 27.8 us; the launch traced here: 27.5 us
  Pallas kernels  26 us (94%)
  local copies, waits for them, and re-layouts  1.49 us (5%)
    pallas_call x1, Pallas kernels, shards(): pl.pallas_call(functools.partial(kernel, n_area, n_depth), out_shape=jax....  26 us
    reshape x1, local copies, waits for them, and re-layouts, shards(): return image.reshape(2, 4, part, columns)  1.49 us

profile of v3, /device:TPU:0, one launch (start us, length us, event | category | flops | bytes accessed | tf_op | source)
XLA Modules:
  0.0 27.5 jit_solution(13903766955439147276)
XLA Ops:
  0.0 26.0 %render.1 = f32[2,16,512]{2,1,0:T(8,128)} custom-call(f32[32,64,512]{2,1,0:T(8,128)} %field_hbm.1, s32[32,64,512]{2,1,0:T(8,128)} %mat_hbm.1, f32[4,16]{1,0:T(4,128)} %tf_hbm.1, s32[2,16]{1,0:T(2,128)} %order_hbm.1, s32[16]{0:T(128)} %shear_hbm.1), custom_call_target="tpu_custom_call" | custom-call | tf_op jit(solution)/shard_map/render/pallas_call | solution.py:535
  26.0 1.5 %reshape.3 = f32[2,4,4,512]{3,2,1,0:T(4,128)} reshape(f32[2,16,512]{2,1,0:T(8,128)} %render.1) | data formatting | bytes 131072 | tf_op jit(solution)/shard_map/reshape | solution.py:571

commit v4 on v3

--- a/solution.py
+++ b/solution.py
@@ -435,17 +435,22 @@
 
         def rest(t, _):
             full(b, [2 * t, 2 * t + 1 + (tiles - 2) * (1 - late)])
+
+            @pl.when(jnp.logical_and(b == early, t == 1))
+            def _():
+                shear(0, recv, (1, 0), a2a_recv.at[1])
+
             return 0
 
         lax.fori_loop(0, 1 + (tiles // 2 - 1) * late, rest, 0)
 
         def finish(t, _):
-            ends(b, [1 + 3 * t + j for j in range(3)])
+            ends(b, [1 + t + j for j in range(inner)])
             return 0
 
-        lax.fori_loop(0, (inner // 3) * (1 - late), finish, 0)
-
-        @pl.when(b > 0)
+        lax.fori_loop(0, 1 - late, finish, 0)
+
+        @pl.when(b >= early)
         def _():
             shear(b - 1, recv, (1, b - 1), a2a_recv.at[1])
 

time: 27.8 us -> 27.5 us (0.989)
  no operation moved by 1% of the time
where the time goes in v4:
time: 27.5 us; the launch traced here: 27.4 us
  Pallas kernels  25.9 us (94%)
  local copies, waits for them, and re-layouts  1.49 us (5%)
    pallas_call x1, Pallas kernels, shards(): pl.pallas_call(functools.partial(kernel, n_area, n_depth), out_shape=jax....  25.9 us
    reshape x1, local copies, waits for them, and re-layouts, shards(): return image.reshape(2, 4, part, columns)  1.49 us

profile of v4, /device:TPU:0, one launch (start us, length us, event | category | flops | bytes accessed | tf_op | source)
XLA Modules:
  0.0 27.4 jit_solution(17383847275403536944)
XLA Ops:
  0.0 25.9 %render.1 = f32[2,16,512]{2,1,0:T(8,128)} custom-call(f32[32,64,512]{2,1,0:T(8,128)} %field_hbm.1, s32[32,64,512]{2,1,0:T(8,128)} %mat_hbm.1, f32[4,16]{1,0:T(4,128)} %tf_hbm.1, s32[2,16]{1,0:T(2,128)} %order_hbm.1, s32[16]{0:T(128)} %shear_hbm.1), custom_call_target="tpu_custom_call" | custom-call | tf_op jit(solution)/shard_map/render/pallas_call | solution.py:540
  25.9 1.5 %reshape.3 = f32[2,4,4,512]{3,2,1,0:T(4,128)} reshape(f32[2,16,512]{2,1,0:T(8,128)} %render.1) | data formatting | bytes 131072 | tf_op jit(solution)/shard_map/reshape | solution.py:576

commit v5 on v4

--- a/solution.py
+++ b/solution.py
@@ -375,7 +375,7 @@
     def early_tile_and_halo(i, _):
         for b in range(1, blocks):
 
-            @pl.when(i == b - 1)
+            @pl.when(i == b)
             def _():
                 if b > 1:
                     wait_field(b)
@@ -433,16 +433,20 @@
         def _():
             wait_mat(b)
 
+        @pl.when(late == 0)
+        def _():
+            full(b, [0, tiles - 1])
+
         def rest(t, _):
-            full(b, [2 * t, 2 * t + 1 + (tiles - 2) * (1 - late)])
-
-            @pl.when(jnp.logical_and(b == early, t == 1))
+            full(b, [4 * t + j for j in range(4)])
+
+            @pl.when(jnp.logical_and(b == early, t == 0))
             def _():
                 shear(0, recv, (1, 0), a2a_recv.at[1])
 
             return 0
 
-        lax.fori_loop(0, 1 + (tiles // 2 - 1) * late, rest, 0)
+        lax.fori_loop(0, (tiles // 4) * late, rest, 0)
 
         def finish(t, _):
             ends(b, [1 + t + j for j in range(inner)])

time: 27.5 us -> 27.5 us (level)
  no operation moved by 1% of the time
where the time goes in v5:
time: 27.5 us; the launch traced here: 27.3 us
  Pallas kernels  25.8 us (94%)
  local copies, waits for them, and re-layouts  1.49 us (5%)
    pallas_call x1, Pallas kernels, shards(): pl.pallas_call(functools.partial(kernel, n_area, n_depth), out_shape=jax....  25.8 us
    reshape x1, local copies, waits for them, and re-layouts, shards(): return image.reshape(2, 4, part, columns)  1.49 us

profile of v5, /device:TPU:0, one launch (start us, length us, event | category | flops | bytes accessed | tf_op | source)
XLA Modules:
  0.0 27.3 jit_solution(11261088586692115451)
XLA Ops:
  0.0 25.8 %render.1 = f32[2,16,512]{2,1,0:T(8,128)} custom-call(f32[32,64,512]{2,1,0:T(8,128)} %field_hbm.1, s32[32,64,512]{2,1,0:T(8,128)} %mat_hbm.1, f32[4,16]{1,0:T(4,128)} %tf_hbm.1, s32[2,16]{1,0:T(2,128)} %order_hbm.1, s32[16]{0:T(128)} %shear_hbm.1), custom_call_target="tpu_custom_call" | custom-call | tf_op jit(solution)/shard_map/render/pallas_call | solution.py:544
  25.8 1.5 %reshape.3 = f32[2,4,4,512]{3,2,1,0:T(4,128)} reshape(f32[2,16,512]{2,1,0:T(8,128)} %render.1) | data formatting | bytes 131072 | tf_op jit(solution)/shard_map/reshape | solution.py:580
